TPU v7x, 512 devices: a whole 4x4x16 slice. The times are simulated.
512 devices in a mesh: node: 32 (over y, z_lo), local: 16 (over x, z_hi, core).
Axes of the slice: x: 4, y: 4, z: 16 (z_hi: 2, z_lo: 8; z = z_hi * 8 + z_lo), core: 2. Of those that a mesh axis runs over, the one named last changes fastest.
Arguments:
- tokens: bfloat16 [65536, 4096], P(('node', 'local')), may hold values from -24 to 24
- key_codes: bfloat16 [4096, 512], P('local'), may hold values from -0.09375 to 0.09375
- key_exponents: int32 [4096, 2], P('local'), may hold values from -1 to 1
- key_cotangent: bfloat16 [65536, 512], P(('node', 'local')), may hold values from -6 to 6
Outputs:
- keys: bfloat16 [65536, 512], P(('node', 'local'))
- input_grad: bfloat16 [65536, 4096], P(('node', 'local'))
- weight_grad: float32 [4096, 512], P(('node', 'local'))
Inputs may be any that keep to these rules, and one draw needn't show every extreme that they name: key_exponents gives the power of two that scales each block of 256 columns of a row of key_codes.
All inputs are finite; a program needn't handle non-finite values.
Results may differ from a plain program's by a relative error of at most 0.015.
Values may be sent and summed in bfloat16 or wider, within the bound.
No kernel may reach another device: no remote copies, remote signals or barrier semaphores. Data moves between devices by JAX's collectives and lax.ppermute only.
A program may use at most 128 MiB of HBM per device.

v0:
```python
import math
import jax
import jax.numpy as jnp
from jax import lax
from jax.sharding import PartitionSpec as P

KVH = 4
HEAD = 128
QBLOCK = 256
SEQ = 8192
THETA = 500000.0


def in_blocks(value, dim, size):
    before, after = (value.shape[:dim], value.shape[dim + 1 :])
    return jnp.moveaxis(value.reshape(*before, size, -1, *after), dim, 0)


def joined_along(blocks, dim):
    blocks = jnp.moveaxis(blocks, 0, dim)
    lengths = blocks.shape
    return blocks.reshape(*lengths[:dim], lengths[dim] * lengths[dim + 1], *lengths[dim + 2 :])


def joined_exchange(value, axis, axes, splits, concats):
    sizes = [lax.axis_size(a) for a in axes]
    blocks = in_blocks(value, splits[0], sizes[0])
    blocks = jnp.moveaxis(in_blocks(blocks, splits[1] + 1, sizes[1]), 0, 1)
    inside = blocks.shape[2:]
    blocks = blocks.reshape(-1, *inside)
    blocks = lax.all_to_all(blocks, axis, split_axis=0, concat_axis=0, tiled=True)
    blocks = joined_along(blocks.reshape(*sizes, *inside), concats[0] + 1)
    return joined_along(blocks, concats[1])


def tables(positions):
    inverse = THETA ** (-(jnp.arange(HEAD // 2, dtype=jnp.float32) * 2.0 / HEAD))
    angles = positions.astype(jnp.float32)[:, None] * inverse[None, :]
    return (jnp.cos(angles), jnp.sin(angles))


def rotate(values, cosine, sine_part):
    count = values.shape[0]
    heads = values.reshape(count, KVH, HEAD)
    first_half = heads[:, :, : HEAD // 2]
    second_half = heads[:, :, HEAD // 2 :]
    cos_rows = cosine[:, None, :]
    sin_rows = sine_part[:, None, :]
    joined = jnp.concatenate(
        [
            first_half * cos_rows - second_half * sin_rows,
            second_half * cos_rows + first_half * sin_rows,
        ],
        axis=2,
    )
    return joined.reshape(count, KVH * HEAD)


def unrotate(values, cosine, sine_part):
    count = values.shape[0]
    heads = values.reshape(count, KVH, HEAD)
    first_half = heads[:, :, : HEAD // 2]
    second_half = heads[:, :, HEAD // 2 :]
    cos_rows = cosine[:, None, :]
    sin_rows = sine_part[:, None, :]
    joined = jnp.concatenate(
        [
            first_half * cos_rows + second_half * sin_rows,
            second_half * cos_rows - first_half * sin_rows,
        ],
        axis=2,
    )
    return joined.reshape(count, KVH * HEAD)


def quantize(partial_value):
    blocks = partial_value.reshape(partial_value.shape[0], partial_value.shape[1] // QBLOCK, QBLOCK)
    largest = jnp.max(jnp.abs(blocks), axis=2)
    block_scale = jnp.exp2(jnp.ceil(jnp.log2(largest + 1e-06)))
    code_values = (blocks / block_scale[:, :, None]).astype(jnp.bfloat16)
    return (code_values, block_scale.astype(jnp.bfloat16))


def expand_codes(code_values, block_scale):
    lead = code_values.shape[:-1]
    blocks = code_values.reshape(lead + (block_scale.shape[-1], QBLOCK))
    values = blocks.astype(jnp.float32) * block_scale.astype(jnp.float32)[..., None]
    return values.reshape(lead + (code_values.shape[-1],))


def on_device(tokens, key_codes, key_exponents, key_cotangent):
    node_count = lax.axis_size("node")
    local_count = lax.axis_size("local")
    tok_count = tokens.shape[0]
    width = tokens.shape[1]
    feature_count = key_codes.shape[1]
    expanded = jnp.repeat(jnp.exp2(key_exponents.astype(jnp.float32)), QBLOCK, axis=1)
    shard_weights = (key_codes.astype(jnp.float32) * expanded).astype(jnp.bfloat16)
    weights = lax.all_gather(shard_weights, "local", axis=0, tiled=True)
    device_index = lax.axis_index("node") * local_count + lax.axis_index("local")
    positions = (device_index * tok_count + jnp.arange(tok_count, dtype=jnp.int32)) % SEQ
    cosine, sine_part = tables(positions)
    pre_grad = unrotate(key_cotangent.astype(jnp.float32), cosine, sine_part).astype(jnp.bfloat16)
    partial_value = lax.dot_general(
        tokens, pre_grad, (((0,), (0,)), ((), ())), preferred_element_type=jnp.float32
    )
    code_values, block_scale = quantize(partial_value)
    row_count = width // (node_count * local_count)
    block_count = feature_count // QBLOCK
    code_grid = code_values.reshape(node_count, local_count, row_count, feature_count)
    scale_grid = block_scale.reshape(node_count, local_count, row_count, block_count)
    projected = jnp.dot(tokens, weights, preferred_element_type=jnp.float32)
    keys = rotate(projected, cosine, sine_part).astype(jnp.bfloat16)
    input_grad = lax.dot_general(
        pre_grad, weights, (((1,), (1,)), ((), ())), preferred_element_type=jnp.float32
    ).astype(jnp.bfloat16)
    got_codes, got_scales = (
        joined_exchange(code_grid, ("local", "node"), ("local", "node"), (1, 0), (1, 0)),
        joined_exchange(scale_grid, ("local", "node"), ("local", "node"), (1, 0), (1, 0)),
    )
    summed = jnp.sum(expand_codes(got_codes, got_scales), axis=(0, 1))
    total_tokens = tok_count * node_count * local_count
    weight_grad = summed * (1.0 / math.sqrt(total_tokens))
    return (keys, input_grad, weight_grad)


def solution(mesh):
    return jax.shard_map(
        on_device,
        mesh=mesh,
        in_specs=(
            P(("node", "local"), None),
            P("local", None),
            P("local", None),
            P(("node", "local"), None),
        ),
        out_specs=(
            P(("node", "local"), None),
            P(("node", "local"), None),
            P(("node", "local"), None),
        ),
        check_vma=False,
    )
```

profile of v0, /device:TPU:1, one launch (start us, length us, event | category | flops | bytes accessed | tf_op | source)
XLA Modules:
  0.0 424.3 jit_solution(15492790936828746594)
XLA Ops:
  7.2 0.0 copy-start
  7.2 0.0 all-gather.2.cloned.1.call-start
  7.2 0.8 multiply_exponential_fusion.1
  8.0 0.1 copy.20
  8.1 0.3 broadcast_in_dim.2
  8.5 1.7 multiply_convert_fusion
  10.3 0.0 all-gather.2.cloned.1.call-update
  10.3 1.0 copy.32
  11.3 0.2 multiply_cosine_fusion
  11.5 125.4 %all-gather.2.cloned.1.call-done = bf16[4096,512]{1,0:T(8,128)(2,1)} async-done(((bf16[256,512]{1,0:T(8,128)(2,1)}), bf16[4096,512]{1,0:T(8,128)(2,1)}) %all-gather.2.cloned.1.call-update) | async-done | bytes 4194320 | tf_op jit(solution)/shard_map/all_gather | solution.py:99
  136.9 0.0 copy-done
  136.9 3.5 fusion.6
  140.4 0.1 add_convert_fusion
  140.5 4.5 %bitcast_reduce_fusion = (f32[4096,2]{0,1:T(2,128)S(1)}, f32[4096,512]{0,1:T(8,128)}) fusion(bf16[128,512]{0,1:T(8,128)(2,1)S(1)} %bitcast.48, bf16[128,4096]{1,0:T(8,128)(2,1)S(1)} %copy-done), kind=kOutput, calls=%fused_computation.3 | convolution fusion | flops 541057024 | bytes 9601024 | tf_op jit(solution)/shard_map/dot_general | solution.py:104
  145.0 0.1 fusion.5
  145.1 0.6 copy.25
  145.7 6.0 %div.25 = f32[4096,2,256]{2,1,0:T(2,128)} broadcast(f32[4096,2]{1,0:T(8,128)S(1)} %copy.25), dimensions={0,1} | broadcast | bytes 8421376 | tf_op jit(solution)/shard_map/div | solution.py:80
  151.7 11.5 %div.26 = f32[32,16,1,8,512]{4,3,1,0,2:T(8,128)} reshape(f32[4096,2,256]{2,1,0:T(2,128)} %div.25) | data formatting | bytes 16777216 | tf_op jit(solution)/shard_map/div | solution.py:80
  163.2 9.0 %copy.24 = f32[4096,512]{1,0:T(8,128)} copy(f32[4096,512]{0,1:T(8,128)} %get-tuple-element.14) | data formatting | bytes 16777216 | tf_op jit(solution)/shard_map/dot_general | solution.py:104
  172.2 0.3 reshape.192
  172.5 1.0 copy.31
  173.5 11.5 %all-to-all-start.1 = ((bf16[512,1,1,8,2]{3,4,2,1,0:T(2,128)(2,1)}), bf16[512,1,1,8,2]{3,4,2,1,0:T(2,128)(2,1)S(1)}, u32[]{:S(2)}, u32[]{:S(2)}) async-start(bf16[512,1,1,8,2]{3,4,2,1,0:T(2,128)(2,1)} %bitcast.14), calls=%async_computation.1 | async-start | bytes 524288 | tf_op jit(solution)/shard_map/all_to_all | solution.py:31
  185.0 7.6 %fusion.2 = bf16[16,32,1,8,512]{4,3,0,1,2:T(8,128)(2,1)S(1)} fusion(f32[32,16,1,8,512]{4,3,1,0,2:T(8,128)} %bitcast.43, f32[32,16,1,8,512]{4,3,1,0,2:T(8,128)} %div.26), kind=kLoop, calls=%fused_computation.7 | loop fusion | flops 4194304 | bytes 20971520 | tf_op jit(solution)/shard_map/transpose | solution.py:16
  192.6 2.4 copy.26
  195.0 14.9 %all-to-all-done.1 = bf16[512,1,1,8,2]{3,4,2,1,0:T(2,128)(2,1)S(1)} async-done(((bf16[512,1,1,8,2]{3,4,2,1,0:T(2,128)(2,1)}), bf16[512,1,1,8,2]{3,4,2,1,0:T(2,128)(2,1)S(1)}, u32[]{:S(2)}, u32[]{:S(2)}) %all-to-all-start.1) | async-done | bytes 16416 | tf_op jit(solution)/shard_map/all_to_all | solution.py:31
  210.0 11.3 %all-to-all-start = ((bf16[512,1,1,8,512]{4,3,2,1,0:T(8,128)(2,1)}), bf16[512,1,1,8,512]{4,3,2,1,0:T(8,128)(2,1)}, u32[]{:S(2)}, u32[]{:S(2)}) async-start(bf16[512,1,1,8,512]{4,3,2,1,0:T(8,128)(2,1)} %bitcast.45), calls=%async_computation | async-start | bytes 8388608 | tf_op jit(solution)/shard_map/all_to_all | solution.py:31
  221.3 0.8 copy.30
  222.1 4.7 %convolution_convert_fusion = bf16[128,4096]{1,0:T(8,128)(2,1)} fusion(bf16[128,512]{0,1:T(8,128)(2,1)S(1)} %bitcast.49, bf16[4096,512]{1,0:T(8,128)(2,1)} %all-gather.2.cloned.1.call-done), kind=kOutput, calls=%fused_computation.6 | convolution fusion | flops 537395200 | bytes 5373952 | tf_op jit(solution)/shard_map/dot_general | solution.py:114
  226.7 0.2 convert_bitcast_fusion.1
  226.9 185.2 %all-to-all-done = bf16[512,1,1,8,512]{4,3,2,1,0:T(8,128)(2,1)} async-done(((bf16[512,1,1,8,512]{4,3,2,1,0:T(8,128)(2,1)}), bf16[512,1,1,8,512]{4,3,2,1,0:T(8,128)(2,1)}, u32[]{:S(2)}, u32[]{:S(2)}) %all-to-all-start) | async-done | bytes 4194336 | tf_op jit(solution)/shard_map/all_to_all | solution.py:31
  412.1 1.2 mul.119
  413.4 0.0 copy-start.1
  413.4 3.4 fusion.1
  416.8 0.6 broadcast_multiply_fusion
  417.4 0.0 copy-done.1
  (4 shorter events, 0.1 us)
Async XLA Ops:
  7.2 129.8 %copy-start = (bf16[128,4096]{1,0:T(8,128)(2,1)S(1)}, bf16[128,4096]{1,0:T(8,128)(2,1)}, u32[]{:S(2)}) copy-start(bf16[128,4096]{1,0:T(8,128)(2,1)} %param.4) | copy-start | bytes 3145732
  7.2 129.7 %all-gather.2.cloned.1.call-start = ((), (), s32[]{:S(2)}) async-start(), calls=%async_computation.2 | async-start | bytes 4456448 | tf_op jit(solution)/shard_map/all_gather | solution.py:99
  173.5 36.5 %all-to-all-start.1 = ((bf16[512,1,1,8,2]{3,4,2,1,0:T(2,128)(2,1)}), bf16[512,1,1,8,2]{3,4,2,1,0:T(2,128)(2,1)S(1)}, u32[]{:S(2)}, u32[]{:S(2)}) async-start(bf16[512,1,1,8,2]{3,4,2,1,0:T(2,128)(2,1)} %bitcast.14), calls=%async_computation.1 | async-start | bytes 524288 | tf_op jit(solution)/shard_map/all_to_all | solution.py:31
  210.0 202.2 %all-to-all-start = ((bf16[512,1,1,8,512]{4,3,2,1,0:T(8,128)(2,1)}), bf16[512,1,1,8,512]{4,3,2,1,0:T(8,128)(2,1)}, u32[]{:S(2)}, u32[]{:S(2)}) async-start(bf16[512,1,1,8,512]{4,3,2,1,0:T(8,128)(2,1)} %bitcast.45), calls=%async_computation | async-start | bytes 8388608 | tf_op jit(solution)/shard_map/all_to_all | solution.py:31
  413.4 4.1 copy-start.1
Sparse Core Ops, SparseCore 0:
  11.9 125.0 all-gather.1
where the time goes:
time: 425 us; the launch traced here: 424 us
  waiting for transfers between devices  326 us (77%)
  local copies, waits for them, and re-layouts  34.4 us (8%)
  starting transfers between devices  22.9 us (5%)
  other arithmetic  14.7 us (3%)
  between operations  14.2 us (3%)
  matrix products  12.6 us (3%)
    all_to_all x2, waiting for transfers between devices, joined_exchange(): lax.all_to_all(blocks, axis, split_axis=0, concat_axis=0, tiled=True)  200 us
    all_gather x1, waiting for transfers between devices, on_device(): weights = lax.all_gather(shard_weights, 'local', axis=0, tiled=True)  125 us
    all_to_all x2, starting transfers between devices, joined_exchange(): lax.all_to_all(blocks, axis, split_axis=0, concat_axis=0, tiled=True)  22.8 us
    div x2, local copies, waits for them, and re-layouts, quantize(): code_values = (blocks / block_scale[:, :, None]).astype(jnp.bfloat16)  17.4 us
    dot_general x1, local copies, waits for them, and re-layouts, on_device(): lax.dot_general(tokens, pre_grad, (((0,), (0,)), ((), ())), preferred_ele...  8.99 us
  transfers between devices with their start and end apart: 3, of which 3 were waited for; matrix products, arithmetic and copies ran while one was open for 4% of the time, Pallas kernels for 0%

commit v1 on v0

--- a/solution.py
+++ b/solution.py
@@ -96,7 +96,9 @@
     feature_count = key_codes.shape[1]
     expanded = jnp.repeat(jnp.exp2(key_exponents.astype(jnp.float32)), QBLOCK, axis=1)
     shard_weights = (key_codes.astype(jnp.float32) * expanded).astype(jnp.bfloat16)
-    weights = lax.all_gather(shard_weights, "local", axis=0, tiled=True)
+    weights = jnp.concatenate(
+        lax.all_to_all(jnp.stack([shard_weights] * lax.axis_size("local")), "local", 0, 0), axis=0
+    )
     device_index = lax.axis_index("node") * local_count + lax.axis_index("local")
     positions = (device_index * tok_count + jnp.arange(tok_count, dtype=jnp.int32)) % SEQ
     cosine, sine_part = tables(positions)

time: 425 us -> 476 us (1.12)
  starting transfers between devices: 22.9 us -> 174 us
  waiting for transfers between devices: 326 us -> 237 us
  between operations: 14.2 us -> 0.89 us
    all_to_all x2, starting transfers between devices: 22.8 us -> 169 us  [joined_exchange(): lax.all_to_all(blocks, axis, split_axis=0, concat_axis=0, tiled=True)]
    all_gather x1 -> x0, waiting for transfers between devices: 125 us -> none  [on_device(): weights = lax.all_gather(shard_weights, 'local', axis=0, tiled=True)]
    all_to_all x0 -> x1, waiting for transfers between devices: none -> 30.7 us  [on_device(): lax.all_to_all(jnp.stack([shard_weights] * lax.axis_size('local')), 'loca...]
    all_to_all x2, waiting for transfers between devices: 200 us -> 206 us  [joined_exchange(): lax.all_to_all(blocks, axis, split_axis=0, concat_axis=0, tiled=True)]
  transfers between devices with their start and end apart: 3 -> 3, of which waited for: 3 -> 3; matrix products, arithmetic and copies ran while one was open for 4% -> 10% of each run, Pallas kernels for 0% -> 0%
where the time goes in v1:
time: 476 us; the launch traced here: 475 us
  waiting for transfers between devices  237 us (50%)
  starting transfers between devices  174 us (37%)
  local copies, waits for them, and re-layouts  38.1 us (8%)
  other arithmetic  12.8 us (3%)
  matrix products  12.6 us (3%)
    all_to_all x2, waiting for transfers between devices, joined_exchange(): lax.all_to_all(blocks, axis, split_axis=0, concat_axis=0, tiled=True)  206 us
    all_to_all x2, starting transfers between devices, joined_exchange(): lax.all_to_all(blocks, axis, split_axis=0, concat_axis=0, tiled=True)  169 us
    all_to_all x1, waiting for transfers between devices, on_device(): lax.all_to_all(jnp.stack([shard_weights] * lax.axis_size('local')), 'loca...  30.7 us
    div x2, local copies, waits for them, and re-layouts, quantize(): code_values = (blocks / block_scale[:, :, None]).astype(jnp.bfloat16)  17.4 us
  transfers between devices with their start and end apart: 3, of which 3 were waited for; matrix products, arithmetic and copies ran while one was open for 10% of the time, Pallas kernels for 0%

profile of v1, /device:TPU:1, one launch (start us, length us, event | category | flops | bytes accessed | tf_op | source)
XLA Modules:
  0.0 475.2 jit_solution(875798948008997446)
XLA Ops:
  0.6 0.0 copy-start
  0.7 1.1 copy.32
  1.8 0.2 multiply_cosine_fusion
  2.0 0.0 copy-start.1
  2.0 0.0 copy-start.3
  2.0 0.5 copy-done.1
  2.6 0.0 copy-done.3
  2.6 0.0 copy-done
  2.6 0.0 copy-start.6
  2.6 0.0 copy-start.5
  2.6 4.5 bitcast_reduce_fusion
  7.1 0.7 fusion.5
  7.8 0.3 reshape.205
  8.1 1.0 copy.31
  9.1 24.3 %all-to-all-start.2 = ((bf16[512,1,1,8,2]{3,4,2,1,0:T(2,128)(2,1)}), bf16[512,1,1,8,2]{3,4,2,1,0:T(2,128)(2,1)S(1)}, u32[]{:S(2)}, u32[]{:S(2)}) async-start(bf16[512,1,1,8,2]{3,4,2,1,0:T(2,128)(2,1)} %bitcast.15), calls=%async_computation.2 | async-start | bytes 524288 | tf_op jit(solution)/shard_map/all_to_all | solution.py:31
  33.4 0.0 copy-done.6
  33.5 0.1 copy.20
  33.6 0.3 broadcast_in_dim.2
  34.0 0.0 copy-done.5
  34.0 0.1 multiply_convert_fusion
  34.1 24.3 %all-to-all-done.2 = bf16[512,1,1,8,2]{3,4,2,1,0:T(2,128)(2,1)S(1)} async-done(((bf16[512,1,1,8,2]{3,4,2,1,0:T(2,128)(2,1)}), bf16[512,1,1,8,2]{3,4,2,1,0:T(2,128)(2,1)S(1)}, u32[]{:S(2)}, u32[]{:S(2)}) %all-to-all-start.2) | async-done | bytes 16416 | tf_op jit(solution)/shard_map/all_to_all | solution.py:31
  58.4 2.3 stack.2
  60.7 4.5 all-to-all-start
  65.2 1.4 copy.25
  66.6 6.0 %div.25 = f32[4096,2,256]{2,1,0:T(2,128)} broadcast(f32[4096,2]{1,0:T(8,128)S(1)} %copy.25), dimensions={0,1} | broadcast | bytes 8421376 | tf_op jit(solution)/shard_map/div | solution.py:80
  72.6 11.5 %div.26 = f32[32,16,1,8,512]{4,3,1,0,2:T(8,128)} reshape(f32[4096,2,256]{2,1,0:T(2,128)} %div.25) | data formatting | bytes 16777216 | tf_op jit(solution)/shard_map/div | solution.py:80
  84.0 9.0 %copy.24 = f32[4096,512]{1,0:T(8,128)} copy(f32[4096,512]{0,1:T(8,128)} %get-tuple-element.12) | data formatting | bytes 16777216 | tf_op jit(solution)/shard_map/dot_general | solution.py:106
  93.0 7.6 %fusion.2 = bf16[16,32,1,8,512]{4,3,0,1,2:T(8,128)(2,1)S(1)} fusion(f32[32,16,1,8,512]{4,3,1,0,2:T(8,128)} %bitcast.44, f32[32,16,1,8,512]{4,3,1,0,2:T(8,128)} %div.26), kind=kLoop, calls=%fused_computation.7 | loop fusion | flops 4194304 | bytes 20971520 | tf_op jit(solution)/shard_map/transpose | solution.py:16
  100.6 2.4 copy.26
  103.0 30.7 %all-to-all-done = bf16[16,256,512]{2,1,0:T(8,128)(2,1)} async-done(((bf16[16,256,512]{2,1,0:T(8,128)(2,1)}), bf16[16,256,512]{2,1,0:T(8,128)(2,1)}, u32[]{:S(2)}, u32[]{:S(2)}) %all-to-all-start) | async-done | bytes 4194336 | tf_op jit(solution)/shard_map/all_to_all | solution.py:100
  133.8 145.0 %all-to-all-start.1 = ((bf16[512,1,1,8,512]{4,3,2,1,0:T(8,128)(2,1)}), bf16[512,1,1,8,512]{4,3,2,1,0:T(8,128)(2,1)}, u32[]{:S(2)}, u32[]{:S(2)}) async-start(bf16[512,1,1,8,512]{4,3,2,1,0:T(8,128)(2,1)} %bitcast.46), calls=%async_computation.1 | async-start | bytes 8388608 | tf_op jit(solution)/shard_map/all_to_all | solution.py:31
  278.7 0.0 copy-start.2
  278.7 0.0 copy-start.4
  278.8 0.2 convert_bitcast_fusion.1
  279.0 3.5 fusion.6
  282.4 0.0 copy-done.2
  282.5 0.0 copy-done.4
  282.5 0.8 copy.30
  283.3 4.6 convolution_convert_fusion
  288.0 182.0 %all-to-all-done.1 = bf16[512,1,1,8,512]{4,3,2,1,0:T(8,128)(2,1)} async-done(((bf16[512,1,1,8,512]{4,3,2,1,0:T(8,128)(2,1)}), bf16[512,1,1,8,512]{4,3,2,1,0:T(8,128)(2,1)}, u32[]{:S(2)}, u32[]{:S(2)}) %all-to-all-start.1) | async-done | bytes 4194336 | tf_op jit(solution)/shard_map/all_to_all | solution.py:31
  470.0 1.2 mul.119
  471.2 3.4 fusion.1
  474.5 0.6 broadcast_multiply_fusion
  (8 shorter events, 0.2 us)
Async XLA Ops:
  0.6 2.0 copy-start
  2.0 0.6 copy-start.1
  2.0 0.6 copy-start.3
  2.6 30.8 %copy-start.6 = (s32[256,2]{0,1:T(2,128)S(1)}, s32[256,2]{0,1:T(2,128)}, u32[]{:S(2)}) copy-start(s32[256,2]{0,1:T(2,128)} %param.6) | copy-start | bytes 6148
  2.6 31.3 %copy-start.5 = (bf16[256,512]{1,0:T(8,128)(2,1)S(1)}, bf16[256,512]{1,0:T(8,128)(2,1)}, u32[]{:S(2)}) copy-start(bf16[256,512]{1,0:T(8,128)(2,1)} %param.5) | copy-start | bytes 786436
  9.1 49.3 %all-to-all-start.2 = ((bf16[512,1,1,8,2]{3,4,2,1,0:T(2,128)(2,1)}), bf16[512,1,1,8,2]{3,4,2,1,0:T(2,128)(2,1)S(1)}, u32[]{:S(2)}, u32[]{:S(2)}) async-start(bf16[512,1,1,8,2]{3,4,2,1,0:T(2,128)(2,1)} %bitcast.15), calls=%async_computation.2 | async-start | bytes 524288 | tf_op jit(solution)/shard_map/all_to_all | solution.py:31
  60.7 73.1 %all-to-all-start = ((bf16[16,256,512]{2,1,0:T(8,128)(2,1)}), bf16[16,256,512]{2,1,0:T(8,128)(2,1)}, u32[]{:S(2)}, u32[]{:S(2)}) async-start(bf16[16,256,512]{2,1,0:T(8,128)(2,1)} %stack.2), calls=%async_computation | async-start | bytes 8388608 | tf_op jit(solution)/shard_map/all_to_all | solution.py:100
  133.8 336.2 %all-to-all-start.1 = ((bf16[512,1,1,8,512]{4,3,2,1,0:T(8,128)(2,1)}), bf16[512,1,1,8,512]{4,3,2,1,0:T(8,128)(2,1)}, u32[]{:S(2)}, u32[]{:S(2)}) async-start(bf16[512,1,1,8,512]{4,3,2,1,0:T(8,128)(2,1)} %bitcast.46), calls=%async_computation.1 | async-start | bytes 8388608 | tf_op jit(solution)/shard_map/all_to_all | solution.py:31
  278.7 3.7 copy-start.2
  278.7 3.7 copy-start.4
